TPU v7x, 32 devices: a whole 2x2x4 slice. The times are simulated.
32 devices in a mesh: group: 2 (over x), row: 16 (over z, y, core).
Axes of the slice: x: 2, y: 2, z: 4, core: 2. Of those that a mesh axis runs over, the one named last changes fastest.
Arguments:
- omega: bfloat16 [51200, 512], P(('group', 'row')), parts along dimension 0, may hold values from -6 to 6
- child_sketch: bfloat16 [102400, 512], P(('group', 'row')), parts along dimension 0, may hold values from -12 to 12
- child_map: int32 [102400], P(('group', 'row')), parts along dimension 0, may hold values from 0 to 25599, as said below
- skel_leaf: int32 [4096], P(('group', 'row')), parts along dimension 0, may hold values from 0 to 1599, as said below
- skel_upper: int32 [16, 128], P('group'), parts along dimension 0, may hold values from 0 to 255, as said below
Outputs:
- interp_leaf: float32 [51200, 128], P(('group', 'row')), parts along dimension 0
- interp_upper: float32 [4096, 128], P(('group', 'row')), parts along dimension 0
- nested_basis: float32 [51200, 128], P(('group', 'row')), parts along dimension 0
There are 2 independent parts, one for each index of `group`. A program takes and returns all parts, laid end to end along the dimension named above; each array names one. Nothing has to cross between parts.
Inputs may be any that keep to these rules, and one draw needn't show every extreme that they name: `child_map`: the rows of each device fall into aligned blocks of 400 rows; all rows of one block name parent rows of a single leaf (one run of 1600 rows), and the blocks of one device name distinct leaves. `skel_leaf`: the 128 numbers of one leaf are distinct local row numbers of that leaf. `skel_upper`: each row holds 128 distinct numbers.
All inputs are finite; a program needn't handle non-finite values.
Results may differ from a plain program's by a relative error of at most 0.0003.
Values may be sent and summed in bfloat16 or wider, within the bound.
A program may use at most 128 MiB of HBM per device.

v0:
```python
import jax
import jax.numpy as jnp
from jax import lax
from jax.sharding import PartitionSpec as P

LINE_CELLS = 400


def extended(block, sides, width):
    for axis, dim in sides:
        count = lax.axis_size(axis)
        forward = [(i, i + 1) for i in range(count - 1)]
        backward = [(target, source) for source, target in forward]
        low = lax.ppermute(
            lax.slice_in_dim(block, block.shape[dim] - width, None, axis=dim), axis, forward
        )
        high = lax.ppermute(lax.slice_in_dim(block, 0, width, axis=dim), axis, backward)
        block = jnp.concatenate([low, block, high], axis=dim)
    return block


def partner_2(value, axis, bit):
    mask = 2**bit
    pairs = [(source, source ^ mask) for source in range(lax.axis_size(axis))]
    return lax.ppermute(value, axis, pairs)


def solve_fit(sketch, chosen):
    gram_matrix = jnp.dot(chosen, chosen.T, precision=lax.Precision.HIGHEST)
    factor = jnp.linalg.cholesky(gram_matrix)
    cross_terms = jnp.dot(sketch, chosen.T, precision=lax.Precision.HIGHEST)
    return jax.scipy.linalg.cho_solve((factor, True), cross_terms.T).T


def local(omega, child_sketch, child_map, skel_leaf, skel_upper):
    rows_dev = omega.shape[0]
    columns = omega.shape[1]
    devices = lax.axis_size("row")
    position = lax.axis_index("row")
    padded = extended(omega, (("row", 0),), LINE_CELLS)
    center = omega.astype(jnp.float32)
    line_above = padded[:rows_dev].astype(jnp.float32)
    line_below = padded[2 * LINE_CELLS :].astype(jnp.float32)
    by_line = center.reshape(rows_dev // LINE_CELLS, LINE_CELLS, columns)
    zero_col = jnp.zeros((rows_dev // LINE_CELLS, 1, columns), jnp.float32)
    left_cell = jnp.concatenate([zero_col, by_line[:, :-1]], axis=1)
    right_cell = jnp.concatenate([by_line[:, 1:], zero_col], axis=1)
    stencil_image = (
        6.0 * center - line_above - line_below - (left_cell + right_cell).reshape(rows_dev, columns)
    )
    slot_count = 4 * rows_dev // devices
    block_count = child_sketch.shape[0] // slot_count
    block_rows = child_sketch.reshape(block_count, slot_count, columns)
    block_maps = child_map.reshape(block_count, slot_count)
    targets = block_maps[:, 0] // rows_dev
    send_rows = jnp.zeros((devices, slot_count, columns), jnp.bfloat16).at[targets].set(block_rows)
    send_maps = jnp.full((devices, slot_count), -1, jnp.int32).at[targets].set(block_maps)
    offset = position * rows_dev
    got_rows, got_maps = (
        lax.all_to_all(send_rows, "row", split_axis=0, concat_axis=0, tiled=True),
        lax.all_to_all(send_maps, "row", split_axis=0, concat_axis=0, tiled=True),
    )
    added = (
        jnp.zeros((rows_dev, columns), jnp.float32)
        .at[jnp.where(got_maps >= 0, got_maps - offset, rows_dev).reshape(-1)]
        .add(got_rows.reshape(-1, columns).astype(jnp.float32), mode="drop")
    )
    sketch = stencil_image + added
    chosen = jnp.take(sketch, skel_leaf, axis=0)
    leaf_fit = solve_fit(sketch, chosen)
    partner = partner_2(chosen, "row", 0)
    is_even = position % 2 == 0
    paired = jnp.where(
        is_even,
        jnp.concatenate([chosen, partner], axis=0),
        jnp.concatenate([partner, chosen], axis=0),
    )
    picked = lax.dynamic_slice_in_dim(skel_upper, position // 2, 1, 0)[0]
    upper_rows = jnp.take(paired, picked, axis=0)
    upper_fit = solve_fit(chosen, upper_rows)
    nested_basis = jnp.dot(leaf_fit, upper_fit, precision=lax.Precision.HIGHEST)
    return (leaf_fit, upper_fit, nested_basis)


def solution(mesh):
    in_specs = (
        P(("group", "row"), None),
        P(("group", "row"), None),
        P(("group", "row")),
        P(("group", "row")),
        P("group", None),
    )
    out_specs = (P(("group", "row"), None), P(("group", "row"), None), P(("group", "row"), None))
    return jax.shard_map(local, mesh=mesh, in_specs=in_specs, out_specs=out_specs, check_vma=False)
```

profile of v0, /device:TPU:19, one launch (start us, length us, event | category | flops | bytes accessed | tf_op | source)
XLA Modules:
  0.0 285.2 jit_solution(16281556508491119110)
XLA Ops:
  0.6 0.8 reshape.145
  1.4 0.1 fusion.26
  1.6 0.6 scatter_custom_fusion
  2.2 0.6 copy.17
  2.9 6.5 %all-to-all-start = ((s32[16,1,400]{2,1,0:T(1,128)}), s32[16,1,400]{2,1,0:T(1,128)S(1)}, u32[]{:S(2)}, u32[]{:S(2)}) async-start(s32[16,1,400]{2,1,0:T(1,128)} %copy.17), calls=%async_computation | async-start | bytes 65536 | tf_op jit(solution)/shard_map/all_to_all | solution.py:61
  9.4 3.3 %broadcast_in_dim.42 = bf16[16,400,512]{2,1,0:T(8,128)(2,1)} broadcast(bf16[]{:T(256)} %constant.125.clone.1), dimensions={} | broadcast | bytes 6553602 | tf_op jit(solution)/shard_map/broadcast_in_dim | solution.py:56
  12.7 8.9 %scatter_fusion = bf16[16,400,512]{2,1,0:T(8,128)(2,1)} fusion(bf16[16,400,512]{2,1,0:T(8,128)(2,1)} %broadcast_in_dim.42, s32[8]{0:T(128)S(1)} %fusion.26, bf16[8,400,512]{2,1,0:T(8,128)(2,1)S(1)} %bitcast.50), kind=kCustom, calls=%fused_computation.3 | custom fusion | bytes 9830432 | tf_op jit(solution)/shard_map/scatter | solution.py:56
  21.7 6.1 %all-to-all-start.1 = ((bf16[16,400,512]{2,1,0:T(8,128)(2,1)}), bf16[16,400,512]{2,1,0:T(8,128)(2,1)}, u32[]{:S(2)}, u32[]{:S(2)}) async-start(bf16[16,400,512]{2,1,0:T(8,128)(2,1)} %scatter_fusion), calls=%async_computation.1 | async-start | bytes 13107200 | tf_op jit(solution)/shard_map/all_to_all | solution.py:60
  27.8 0.1 fusion.31
  27.9 2.3 collective-permute-start.1
  30.1 3.3 %collective-permute-start = (bf16[400,512]{1,0:T(8,128)(2,1)S(1)}, bf16[400,512]{1,0:T(8,128)(2,1)S(1)}, u32[]{:S(2)}, u32[]{:S(2)}) collective-permute-start(bf16[400,512]{1,0:T(8,128)(2,1)S(1)} %get-tuple-element.16), channel_id=1, source_target_pairs={{0,1},{1,2},{2,3},{3,4},{4,5},{5,6},{6,7},{7,8},{8,9},{9,10},{10,1... | collective-permute-start | bytes 1228808 | tf_op jit(solution)/shard_map/ppermute | solution.py:14
  33.5 0.7 fusion.28
  34.2 0.7 compare_and_fusion
  34.9 0.9 fusion.32
  35.8 2.5 pad_add_fusion
  38.3 0.1 fusion.22
  38.4 0.1 select_n.93
  38.5 0.1 fusion.23
  38.6 31.4 %collective-permute-done.1 = bf16[400,512]{1,0:T(8,128)(2,1)S(1)} collective-permute-done((bf16[400,512]{1,0:T(8,128)(2,1)S(1)}, bf16[400,512]{1,0:T(8,128)(2,1)S(1)}, u32[]{:S(2)}, u32[]{:S(2)}) %collective-permute-start.1) | collective-permute-done | bytes 409632 | tf_op jit(solution)/shard_map/ppermute | solution.py:17
  70.0 0.0 collective-permute-done
  70.0 4.5 %bitcast_subtract_fusion = f32[1600,512]{1,0:T(8,128)} fusion(f32[4,400,512]{2,1,0:T(8,128)} %pad_add_fusion, bf16[400,512]{1,0:T(8,128)(2,1)S(1)} %collective-permute-done.1, bf16[1600,512]{1,0:T(8,128)(2,1)S(1)} %copy-done, bf16[400,512]{1,0:T(8,128)(2,1)S(1)} %collective-permute-done), kind=kLoop, calls=%fused_computation.7 | loop fusion | flops 10649600 | bytes 9011200 | tf_op jit(solution)/shard_map/sub | solution.py:49
  74.5 96.0 %all-to-all-done.1 = bf16[16,400,512]{2,1,0:T(8,128)(2,1)} async-done(((bf16[16,400,512]{2,1,0:T(8,128)(2,1)}), bf16[16,400,512]{2,1,0:T(8,128)(2,1)}, u32[]{:S(2)}, u32[]{:S(2)}) %all-to-all-start.1) | async-done | bytes 6553632 | tf_op jit(solution)/shard_map/all_to_all | solution.py:60
  170.5 44.5 %scatter_custom_fusion.2 = f32[1600,512]{1,0:T(8,128)} fusion(f32[1600,512]{1,0:T(8,128)} %bitcast_subtract_fusion, s32[6400]{0:T(1024)S(1)} %fusion.23, bf16[6400,512]{1,0:T(8,128)(2,1)} %bitcast.16), kind=kCustom, calls=%fused_computation.5 | custom fusion | flops 6553600 | bytes 9830400 | tf_op jit(solution)/shard_map/scatter-add | solution.py:66
  215.0 2.8 gather_fusion
  217.8 0.1 broadcast_select_fusion
  217.9 4.7 %fusion.34 = f32[128,1600]{0,1:T(8,128)S(1)} fusion(f32[128,512]{1,0:T(8,128)S(1)} %broadcast_select_fusion, f32[1600,512]{1,0:T(8,128)} %scatter_custom_fusion.2), kind=kOutput, calls=%fused_computation.69 | convolution fusion | flops 1258291200 | bytes 4358144 | tf_op jit(solution)/shard_map/dot_general | solution.py:31
  222.6 0.4 fusion.33
  223.0 9.7 %collective-permute-start.2 = (f32[128,512]{1,0:T(8,128)S(1)}, f32[128,512]{1,0:T(8,128)S(1)}, u32[]{:S(2)}, u32[]{:S(2)}) collective-permute-start(f32[128,512]{1,0:T(8,128)S(1)} %broadcast_select_fusion), channel_id=1, source_target_pairs={{0,1},{1,0},{2,3},{3,2},{4,5},{5,4},{6,7},{7,6},{8,9},{9,8},{10,11... | collective-permute-start | bytes 786440 | tf_op jit(solution)/shard_map/ppermute | solution.py:25
  232.7 0.1 copy.18
  232.8 11.7 %cholesky.44 = f32[128,128]{1,0:T(8,128)S(1)} custom-call(f32[128,128]{1,0:T(8,128)S(1)} %fusion.21), custom_call_target="Cholesky" | custom-call | tf_op jit(solution)/shard_map/jit(cholesky)/cholesky | solution.py:30
  244.5 0.6 compare_reduce_fusion.1
  245.2 0.7 fusion.10
  245.8 9.8 %custom-call.16 = f32[1,128,128]{1,2,0:T(8,128)S(1)} custom-call(f32[1,128,128]{2,1,0:T(8,128)S(1)} %fusion.10), custom_call_target="InvertDiagBlocksLowerTriangular" | custom-call | tf_op jit(solution)/shard_map/jit(_cho_solve)/triangular_solve | solution.py:32
  255.6 0.8 fusion.19
  256.5 0.8 fusion.17
  257.3 0.0 copy-start.2
  257.4 0.8 gather_fusion.1
  258.1 0.4 fusion.2
  258.5 0.7 fusion.4
  259.3 0.1 copy.19
  259.4 11.7 %cholesky.55 = f32[128,128]{1,0:T(8,128)S(1)} custom-call(f32[128,128]{1,0:T(8,128)S(1)} %fusion.16), custom_call_target="Cholesky" | custom-call | tf_op jit(solution)/shard_map/jit(cholesky)/cholesky | solution.py:30
  271.1 0.6 compare_reduce_fusion
  271.8 0.7 fusion.11
  272.4 9.8 %custom-call.17 = f32[1,128,128]{1,2,0:T(8,128)S(1)} custom-call(f32[1,128,128]{2,1,0:T(8,128)S(1)} %fusion.11), custom_call_target="InvertDiagBlocksLowerTriangular" | custom-call | tf_op jit(solution)/shard_map/jit(_cho_solve)/triangular_solve | solution.py:32
  282.2 0.3 fusion.14
  282.5 0.2 fusion.12
  282.7 0.7 copy.20
  283.5 1.7 fusion.35
  (18 shorter events, 0.2 us)
Async XLA Ops:
  2.9 18.8 %all-to-all-start = ((s32[16,1,400]{2,1,0:T(1,128)}), s32[16,1,400]{2,1,0:T(1,128)S(1)}, u32[]{:S(2)}, u32[]{:S(2)}) async-start(s32[16,1,400]{2,1,0:T(1,128)} %copy.17), calls=%async_computation | async-start | bytes 65536 | tf_op jit(solution)/shard_map/all_to_all | solution.py:61
  9.4 3.3 %copy-start.1 = (bf16[3200,512]{1,0:T(8,128)(2,1)S(1)}, bf16[3200,512]{1,0:T(8,128)(2,1)}, u32[]{:S(2)}) copy-start(bf16[3200,512]{1,0:T(8,128)(2,1)} %param.7) | copy-start | bytes 9830404
  21.7 6.1 %copy-start = (bf16[1600,512]{1,0:T(8,128)(2,1)S(1)}, bf16[1600,512]{1,0:T(8,128)(2,1)}, u32[]{:S(2)}) copy-start(bf16[1600,512]{1,0:T(8,128)(2,1)} %param.6) | copy-start | bytes 4915204
  21.7 13.2 %copy-start.3 = (s32[128]{0:T(128)S(1)}, s32[128]{0:T(128)}, u32[]{:S(2)}) copy-start(s32[128]{0:T(128)} %param.9) | copy-start | bytes 1540
  21.7 148.9 %all-to-all-start.1 = ((bf16[16,400,512]{2,1,0:T(8,128)(2,1)}), bf16[16,400,512]{2,1,0:T(8,128)(2,1)}, u32[]{:S(2)}, u32[]{:S(2)}) async-start(bf16[16,400,512]{2,1,0:T(8,128)(2,1)} %scatter_fusion), calls=%async_computation.1 | async-start | bytes 13107200 | tf_op jit(solution)/shard_map/all_to_all | solution.py:60
  27.9 42.2 %collective-permute-start.1 = (bf16[400,512]{1,0:T(8,128)(2,1)S(1)}, bf16[400,512]{1,0:T(8,128)(2,1)S(1)}, u32[]{:S(2)}, u32[]{:S(2)}) collective-permute-start(bf16[400,512]{1,0:T(8,128)(2,1)S(1)} %get-tuple-element.17), channel_id=1, source_target_pairs={{1,0},{2,1},{3,2},{4,3},{5,4},{6,5},{7,6},{8,7},{9,8},{10,9},{11,1... | collective-permute-start | bytes 1228808 | tf_op jit(solution)/shard_map/ppermute | solution.py:17
  30.1 39.9 %collective-permute-start = (bf16[400,512]{1,0:T(8,128)(2,1)S(1)}, bf16[400,512]{1,0:T(8,128)(2,1)S(1)}, u32[]{:S(2)}, u32[]{:S(2)}) collective-permute-start(bf16[400,512]{1,0:T(8,128)(2,1)S(1)} %get-tuple-element.16), channel_id=1, source_target_pairs={{0,1},{1,2},{2,3},{3,4},{4,5},{5,6},{6,7},{7,8},{8,9},{9,10},{10,1... | collective-permute-start | bytes 1228808 | tf_op jit(solution)/shard_map/ppermute | solution.py:14
  223.0 34.3 %collective-permute-start.2 = (f32[128,512]{1,0:T(8,128)S(1)}, f32[128,512]{1,0:T(8,128)S(1)}, u32[]{:S(2)}, u32[]{:S(2)}) collective-permute-start(f32[128,512]{1,0:T(8,128)S(1)} %broadcast_select_fusion), channel_id=1, source_target_pairs={{0,1},{1,0},{2,3},{3,2},{4,5},{5,4},{6,7},{7,6},{8,9},{9,8},{10,11... | collective-permute-start | bytes 786440 | tf_op jit(solution)/shard_map/ppermute | solution.py:25
  257.3 27.9 %copy-start.2 = (f32[128,1600]{0,1:T(8,128)}, f32[128,1600]{0,1:T(8,128)S(1)}, u32[]{:S(2)}) copy-start(f32[128,1600]{0,1:T(8,128)S(1)} %fusion.17) | copy-start | bytes 2457604
where the time goes:
time: 286 us; the launch traced here: 285 us
  waiting for transfers between devices  127 us (44%)
  other arithmetic  99 us (35%)
  starting transfers between devices  27.9 us (10%)
  local copies, waits for them, and re-layouts  19.9 us (7%)
  matrix products  9.99 us (3%)
    all_to_all x1, waiting for transfers between devices, local(): lax.all_to_all(send_rows, 'row', split_axis=0, concat_axis=0, tiled=True)  96 us
    scatter-add x1, other arithmetic, local(): added = jnp.zeros((rows_dev, columns), jnp.float32).at[jnp.where(got_maps...  44.5 us
    ppermute x1, waiting for transfers between devices, extended(): lax.ppermute(lax.slice_in_dim(block, 0, width, axis=dim), axis, backward)  31.4 us
    another operation x6, other arithmetic, solve_fit(): factor = jnp.linalg.cholesky(gram_matrix)  24.8 us
    another operation x4, other arithmetic, solve_fit(): return jax.scipy.linalg.cho_solve((factor, True), cross_terms.T).T  20.9 us
    ppermute x1, starting transfers between devices, partner_2(): return lax.ppermute(value, axis, pairs)  9.7 us
    scatter x1, local copies, waits for them, and re-layouts, local(): jnp.zeros((devices, slot_count, columns), jnp.bfloat16).at[targets]  8.95 us
    all_to_all x1, starting transfers between devices, local(): lax.all_to_all(send_maps, 'row', split_axis=0, concat_axis=0, tiled=True)  6.5 us
  transfers between devices with their start and end apart: 5, of which 2 were waited for; matrix products, arithmetic and copies ran while one was open for 16% of the time, Pallas kernels for 0%

commit v1 on v0

v1 whole, which is shorter than its diff:
```python
import functools

import jax
import jax.numpy as jnp
from jax import lax
from jax.experimental import pallas as pl
from jax.experimental.pallas import tpu as pltpu
from jax.sharding import PartitionSpec as P

LINE_CELLS = 400
MESH = pl.DeviceIdType.MESH
HIGHEST = lax.Precision.HIGHEST


def exact_dot(left, right):
    return jnp.dot(left, right, precision=HIGHEST, preferred_element_type=jnp.float32)


def dot_rows(left, right):
    return lax.dot_general(
        left, right, (((1,), (1,)), ((), ())), precision=HIGHEST, preferred_element_type=jnp.float32
    )


def front_kernel(
    n, inv_ref, skel_ref, child_ref, map_ref, omega_ref, cross_ref, pair_ref,
    send_rows, got_rows, send_maps, got_maps, halo, sketch, chosen,
    row_send, row_recv, map_send, map_recv, halo_send, halo_recv, pair_send, pair_recv,
):
    me = lax.axis_index("row")
    rows = sketch.shape[0]
    columns = sketch.shape[1]
    rank = chosen.shape[1]
    tile = LINE_CELLS
    parity = me % 2
    partner = me + 1 - 2 * parity

    halo[...] = jnp.zeros_like(halo)
    barrier = pltpu.get_barrier_semaphore()

    def greet(j, carry):
        pl.semaphore_signal(barrier, inc=1, device_id={"row": (me + j) % n}, device_id_type=MESH)
        return carry

    lax.fori_loop(1, n, greet, 0)
    pl.semaphore_wait(barrier, n - 1)

    def distance(i):
        return (n // 2 + (1 - 2 * (i % 2)) * (i // 2)) % n

    def row_copy(j):
        return pltpu.make_async_remote_copy(
            send_rows.at[j], got_rows.at[j], row_send.at[j], row_recv.at[j],
            device_id={"row": (me + j) % n}, device_id_type=MESH,
        )

    def map_copy(j):
        return pltpu.make_async_remote_copy(
            send_maps.at[j], got_maps.at[j], map_send.at[j], map_recv.at[j],
            device_id={"row": (me + j) % n}, device_id_type=MESH,
        )

    def halo_copy(side):
        start = rows - LINE_CELLS if side == 0 else 0
        return pltpu.make_async_remote_copy(
            omega_ref.at[pl.ds(start, LINE_CELLS)], halo.at[side], halo_send.at[side], halo_recv.at[side],
            device_id={"row": (me + 1) % n if side == 0 else (me + n - 1) % n}, device_id_type=MESH,
        )

    def local_map(to):
        block = inv_ref[to]
        return jnp.where(block >= 0, map_ref[jnp.maximum(block, 0)] - to * rows, -1)

    def send(i, carry):
        j = distance(i)
        to = (me + j) % n
        send_maps[j] = local_map(to)
        map_copy(j).start()
        send_rows[j] = child_ref[jnp.maximum(inv_ref[to], 0)]
        row_copy(j).start()
        return carry

    @pl.when(me < n - 1)
    def _():
        halo_copy(0).start()

    @pl.when(me > 0)
    def _():
        halo_copy(1).start()

    lax.fori_loop(1, n, send, 0)

    @pl.when(me < n - 1)
    def _():
        halo_copy(0).wait_send()
        halo_copy(1).wait_recv()

    @pl.when(me > 0)
    def _():
        halo_copy(1).wait_send()
        halo_copy(0).wait_recv()

    cell = lax.broadcasted_iota(jnp.int32, (LINE_CELLS, columns), 0)
    lines = rows // LINE_CELLS
    for line in range(lines):
        here = omega_ref[line * LINE_CELLS:(line + 1) * LINE_CELLS].astype(jnp.float32)
        above = halo[0] if line == 0 else omega_ref[(line - 1) * LINE_CELLS:line * LINE_CELLS]
        below = halo[1] if line == lines - 1 else omega_ref[(line + 1) * LINE_CELLS:(line + 2) * LINE_CELLS]
        left = jnp.where(cell == 0, 0.0, pltpu.roll(here, 1, 0))
        right = jnp.where(cell == LINE_CELLS - 1, 0.0, pltpu.roll(here, LINE_CELLS - 1, 0))
        sketch[line * LINE_CELLS:(line + 1) * LINE_CELLS] = (
            6.0 * here - above.astype(jnp.float32) - below.astype(jnp.float32) - left - right
        )

    def extend_add(numbers, block):
        def step(t, carry):
            start = pl.multiple_of(t * tile, 16)
            row = lax.broadcasted_iota(jnp.int32, (tile, numbers.shape[1]), 0) + start
            hot = (row == numbers).astype(jnp.float32).astype(jnp.bfloat16)
            sketch[pl.ds(start, tile)] += jnp.dot(hot, block, preferred_element_type=jnp.float32)
            return carry

        lax.fori_loop(0, rows // tile, step, 0)

    extend_add(local_map(me), child_ref[jnp.maximum(inv_ref[me], 0)])

    def receive(i, carry):
        j = distance(i)
        map_copy(j).wait()
        row_copy(j).wait()
        extend_add(got_maps[j], got_rows[j])
        return carry

    lax.fori_loop(1, n, receive, 0)

    def choose(i, carry):
        for u in range(8):
            chosen[parity, pl.ds(i * 8 + u, 1), :] = sketch[pl.ds(skel_ref[i * 8 + u], 1), :]
        return carry

    lax.fori_loop(0, rank // 8, choose, 0)
    pair_copy = pltpu.make_async_remote_copy(
        chosen.at[parity], chosen.at[parity], pair_send, pair_recv,
        device_id={"row": partner}, device_id_type=MESH,
    )
    pair_copy.start()
    own = chosen[parity]

    def cross(t, carry):
        start = pl.multiple_of(t * tile, 16)
        cross_ref[pl.ds(start, tile)] = dot_rows(sketch[pl.ds(start, tile)], own)
        return carry

    lax.fori_loop(0, rows // tile, cross, 0)
    pair_copy.wait()
    pair_ref[...] = chosen[...]


def invert_pair(first, second):
    size = first.shape[0]
    row_id = lax.broadcasted_iota(jnp.int32, (size, size), 0)
    lane_id = lax.broadcasted_iota(jnp.int32, (size, size), 1)
    matrices = [first, second]
    for k in range(size):
        for m in range(2):
            a = matrices[m]
            scale = 1.0 / a[k:k + 1, k:k + 1]
            row = jnp.where(lane_id[:1] == k, 1.0, a[k:k + 1, :]) * scale
            column = a[:, k:k + 1]
            rest = jnp.where(lane_id == k, 0.0, a) - column * row
            matrices[m] = jnp.where(row_id == k, row, rest)
    return matrices


def solve_kernel(pick_ref, side_ref, cross_ref, pair_ref, leaf_ref, upper_ref, nested_ref, picked):
    rank = picked.shape[0]
    own = pair_ref[pl.ds(pl.multiple_of(side_ref[0] * rank, rank), rank), :]

    def pick(i, carry):
        for u in range(8):
            picked[pl.ds(i * 8 + u, 1), :] = pair_ref[pl.ds(pick_ref[i * 8 + u], 1), :]
        return carry

    lax.fori_loop(0, rank // 8, pick, 0)
    upper_rows = picked[...]
    leaf_inverse, upper_inverse = invert_pair(dot_rows(own, own), dot_rows(upper_rows, upper_rows))
    upper = exact_dot(dot_rows(own, upper_rows), upper_inverse)
    upper_ref[...] = upper
    tile = LINE_CELLS

    def finish(t, carry):
        start = pl.multiple_of(t * tile, 16)
        terms = cross_ref[pl.ds(start, tile)]
        leaf = exact_dot(terms, leaf_inverse)
        leaf_ref[pl.ds(start, tile)] = leaf
        nested_ref[pl.ds(start, tile)] = exact_dot(leaf, upper)
        return carry

    lax.fori_loop(0, cross_ref.shape[0] // tile, finish, 0)


def local(omega, child_sketch, child_map, skel_leaf, skel_upper):
    rows, columns = omega.shape
    rank = skel_leaf.shape[0]
    n = lax.axis_size("row")
    position = lax.axis_index("row")
    slot = 4 * rows // n
    blocks = child_sketch.shape[0] // slot
    padded = -(-slot // 16) * 16
    child = child_sketch.reshape(blocks, slot, columns)
    maps = child_map.reshape(blocks, 1, slot)
    targets = maps[:, 0, 0] // rows
    if padded != slot:
        child = jnp.pad(child, ((0, 0), (0, padded - slot), (0, 0)))
        maps = jnp.pad(maps, ((0, 0), (0, 0), (0, padded - slot)), constant_values=-1)
    numbers = jnp.arange(blocks, dtype=jnp.int32)
    places = jnp.arange(n, dtype=jnp.int32)
    inv = jnp.max(jnp.where(targets[None, :] == places[:, None], numbers[None, :], -1), axis=1)
    vmem = pl.BlockSpec(memory_space=pltpu.VMEM)
    smem = pl.BlockSpec(memory_space=pltpu.SMEM)
    dma = pltpu.SemaphoreType.DMA
    cross, pair = pl.pallas_call(
        functools.partial(front_kernel, n),
        out_shape=(
            jax.ShapeDtypeStruct((rows, rank), jnp.float32),
            jax.ShapeDtypeStruct((2, rank, columns), jnp.float32),
        ),
        in_specs=[smem, smem, vmem, vmem, vmem],
        out_specs=(vmem, vmem),
        scratch_shapes=[
            pltpu.VMEM((n, padded, columns), jnp.bfloat16),
            pltpu.VMEM((n, padded, columns), jnp.bfloat16),
            pltpu.VMEM((n, 1, padded), jnp.int32),
            pltpu.VMEM((n, 1, padded), jnp.int32),
            pltpu.VMEM((2, LINE_CELLS, columns), jnp.bfloat16),
            pltpu.VMEM((rows, columns), jnp.float32),
            pltpu.VMEM((2, rank, columns), jnp.float32),
            dma((n,)), dma((n,)), dma((n,)), dma((n,)), dma((2,)), dma((2,)), dma, dma,
        ],
        compiler_params=pltpu.CompilerParams(
            collective_id=0, has_side_effects=True, vmem_limit_bytes=48 * 1024 * 1024
        ),
    )(inv, skel_leaf, child, maps, omega)
    picks = lax.dynamic_slice_in_dim(skel_upper, position // 2, 1, 0)[0]
    return pl.pallas_call(
        solve_kernel,
        out_shape=(
            jax.ShapeDtypeStruct((rows, rank), jnp.float32),
            jax.ShapeDtypeStruct((rank, rank), jnp.float32),
            jax.ShapeDtypeStruct((rows, rank), jnp.float32),
        ),
        in_specs=[smem, smem, vmem, vmem],
        out_specs=(vmem, vmem, vmem),
        scratch_shapes=[pltpu.VMEM((rank, columns), jnp.float32)],
        compiler_params=pltpu.CompilerParams(vmem_limit_bytes=32 * 1024 * 1024),
    )(picks, (position % 2).reshape(1), cross, pair.reshape(2 * rank, columns))


def solution(mesh):
    in_specs = (
        P(("group", "row"), None),
        P(("group", "row"), None),
        P(("group", "row")),
        P(("group", "row")),
        P("group", None),
    )
    out_specs = (P(("group", "row"), None), P(("group", "row"), None), P(("group", "row"), None))
    return jax.shard_map(local, mesh=mesh, in_specs=in_specs, out_specs=out_specs, check_vma=False)
```

time: 286 us -> 186 us (0.65)
  the two profiles are of different devices: /device:TPU:19 before, /device:TPU:13 now
where the time goes in v1:
time: 186 us
  Pallas kernels  181 us (97%)
  local copies, waits for them, and re-layouts  3.56 us (2%)
    pallas_call x1, Pallas kernels, local(): pl.pallas_call(functools.partial(front_kernel, n), out_shape=(jax.ShapeDt...  164 us
    pallas_call x1, Pallas kernels, local(): pl.pallas_call(solve_kernel, out_shape=(jax.ShapeDtypeStruct((rows, rank)...  16.8 us

profile of v1, /device:TPU:13, one launch (start us, length us, event | category | flops | bytes accessed | tf_op | source)
XLA Modules:
  0.0 186.1 jit_solution(9264656832444159840)
XLA Ops:
  0.6 0.0 copy-start
  0.7 0.7 copy-done
  1.3 0.8 reshape.47.map_ref
  2.1 0.2 and_reduce_fusion
  2.4 0.2 divide_reduce_fusion
  2.6 0.1 select_reduce_fusion.inv_ref
  2.7 0.0 copy-start.1
  2.7 1.4 copy-done.1
  4.2 0.0 copy-start.2
  4.2 0.7 copy-done.2
  4.8 164.4 %shard_map.76 = (f32[1600,128]{1,0:T(8,128)S(1)}, f32[2,128,512]{2,1,0:T(8,128)S(1)}) custom-call(s32[16]{0:T(128)S(1)} %select_reduce_fusion.inv_ref, s32[128]{0:T(128)S(1)} %copy-done.2, bf16[8,400,512]{2,1,0:T(8,128)(2,1)} %bitcast.6, s32[8,1,400]{2,1,0:T(1,128)S(1)} %reshape.47.map_ref, bf16[1600,512]{1,0:T(8,128)(2,1)S(1)} %copy-done.1), custom_call_target="tpu_custom_call" | custom-call | tf_op jit(solution)/shard_map/pallas_call | solution.py:222
  169.3 16.8 %shard_map.77 = (f32[1600,128]{1,0:T(8,128)}, f32[128,128]{1,0:T(8,128)}, f32[1600,128]{1,0:T(8,128)}) custom-call(s32[128]{0:T(128)S(1)} %dynamic-slice_bitcast_fusion.pick_ref, s32[1]{0:T(128)} %bitcast.1.side_ref, f32[1600,128]{1,0:T(8,128)S(1)} %get-tuple-element.5.cross_ref, f32[256,512]{1,0:T(8,128)S(1)} %bitcast.5), custom_call_target="tpu_custom_call" | custom-call | tf_op jit(solution)/shard_map/pallas_call | solution.py:245
  (2 shorter events, 0.0 us)
Async XLA Ops:
  0.6 0.7 copy-start
  2.7 1.4 copy-start.1
  4.2 0.7 copy-start.2

commit v2 on v1

--- a/solution.py
+++ b/solution.py
@@ -8,6 +8,9 @@
 from jax.sharding import PartitionSpec as P
 
 LINE_CELLS = 400
+LANES = 128
+TILE = 320
+GROUP = 64
 MESH = pl.DeviceIdType.MESH
 HIGHEST = lax.Precision.HIGHEST
 
@@ -24,18 +27,27 @@
 
 def front_kernel(
     n, inv_ref, skel_ref, child_ref, map_ref, omega_ref, cross_ref, pair_ref,
-    send_rows, got_rows, send_maps, got_maps, halo, sketch, chosen,
-    row_send, row_recv, map_send, map_recv, halo_send, halo_recv, pair_send, pair_recv,
+    own_rows, got_own, far_rows, got_far, send_maps, got_maps, hot, coded, got_coded, scales, got_scales,
+    halo, sketch, chosen,
+    own_send, own_recv, far_send, far_recv, map_send, map_recv,
+    code_send, code_recv, scale_send, scale_recv, halo_send, halo_recv, pair_send, pair_recv,
 ):
     me = lax.axis_index("row")
     rows = sketch.shape[0]
     columns = sketch.shape[1]
     rank = chosen.shape[1]
-    tile = LINE_CELLS
+    padded = child_ref.shape[1]
+    half = n // 2
+    base = me // half * half
+    place = me % half
+    mirror = (me + half) % n
+    other = mirror // half * half
     parity = me % 2
     partner = me + 1 - 2 * parity
+    chunks = columns // LANES
 
     halo[...] = jnp.zeros_like(halo)
+    scales[...] = jnp.zeros_like(scales)
     barrier = pltpu.get_barrier_semaphore()
 
     def greet(j, carry):
@@ -45,19 +57,31 @@
     lax.fori_loop(1, n, greet, 0)
     pl.semaphore_wait(barrier, n - 1)
 
-    def distance(i):
-        return (n // 2 + (1 - 2 * (i % 2)) * (i // 2)) % n
-
-    def row_copy(j):
+    def peer_copy(source, target, send, recv, j):
         return pltpu.make_async_remote_copy(
-            send_rows.at[j], got_rows.at[j], row_send.at[j], row_recv.at[j],
-            device_id={"row": (me + j) % n}, device_id_type=MESH,
-        )
+            source, target, send, recv,
+            device_id={"row": base + (place + j) % half}, device_id_type=MESH,
+        )
+
+    def own_copy(j):
+        return peer_copy(own_rows.at[j], got_own.at[j], own_send.at[j], own_recv.at[j], j)
+
+    def far_copy(q, j):
+        return peer_copy(far_rows.at[q, j], got_far.at[q, j], far_send.at[q, j], far_recv.at[q, j], j)
 
     def map_copy(j):
+        return peer_copy(send_maps.at[j], got_maps.at[j], map_send.at[j], map_recv.at[j], j)
+
+    def code_copy(q):
         return pltpu.make_async_remote_copy(
-            send_maps.at[j], got_maps.at[j], map_send.at[j], map_recv.at[j],
-            device_id={"row": (me + j) % n}, device_id_type=MESH,
+            coded.at[q], got_coded.at[q], code_send.at[q], code_recv.at[q],
+            device_id={"row": mirror}, device_id_type=MESH,
+        )
+
+    def scale_copy(q):
+        return pltpu.make_async_remote_copy(
+            scales.at[q], got_scales.at[q], scale_send.at[q], scale_recv.at[q],
+            device_id={"row": mirror}, device_id_type=MESH,
         )
 
     def halo_copy(side):
@@ -71,14 +95,35 @@
         block = inv_ref[to]
         return jnp.where(block >= 0, map_ref[jnp.maximum(block, 0)] - to * rows, -1)
 
-    def send(i, carry):
-        j = distance(i)
-        to = (me + j) % n
-        send_maps[j] = local_map(to)
+    def block_of(to):
+        return jnp.maximum(inv_ref[to], 0)
+
+    def send_map(j, carry):
+        at = (place + j) % half
+        send_maps[j, 0] = local_map(base + at)
+        send_maps[j, 1] = local_map(other + at)
         map_copy(j).start()
-        send_rows[j] = child_ref[jnp.maximum(inv_ref[to], 0)]
-        row_copy(j).start()
-        return carry
+        return carry
+
+    def send_far(q):
+        def step(j, carry):
+            far_rows[q, j] = child_ref[block_of(other + (place + j) % half), :, q * LANES:(q + 1) * LANES]
+            far_copy(q, j).start()
+            return carry
+
+        lax.fori_loop(1, half, step, 0)
+
+    def send_own(j, carry):
+        own_rows[j] = child_ref[block_of(base + (place + j) % half)]
+        own_copy(j).start()
+        return carry
+
+    def send_group(g):
+        low, high = 1 + (half - 1) * g // chunks, 1 + (half - 1) * (g + 1) // chunks
+        lax.fori_loop(low, high, send_own, 0)
+
+    lax.fori_loop(1, half, send_map, 0)
+    send_far(0)
 
     @pl.when(me < n - 1)
     def _():
@@ -88,7 +133,67 @@
     def _():
         halo_copy(1).start()
 
-    lax.fori_loop(1, n, send, 0)
+    for q in range(1, chunks):
+        send_far(q)
+    send_group(0)
+
+    def mark(j, numbers):
+        def step(t, carry):
+            start = pl.multiple_of(t * TILE, 16)
+            row = lax.broadcasted_iota(jnp.int32, (TILE, padded), 0) + start
+            hot[j, pl.ds(start, TILE)] = (row == numbers).astype(jnp.float32).astype(jnp.bfloat16)
+            return carry
+
+        lax.fori_loop(0, rows // TILE, step, 0)
+
+    mark(0, local_map(mirror))
+    far_block = block_of(mirror)
+    for q in range(chunks):
+        got_far[q, 0] = child_ref[far_block, :, q * LANES:(q + 1) * LANES]
+
+    def mark_peer(j, carry):
+        map_copy(j).wait()
+        mark(j, got_maps[j, 1])
+        return carry
+
+    lax.fori_loop(1, half, mark_peer, 0)
+
+    eye = (
+        lax.broadcasted_iota(jnp.int32, (GROUP, LANES), 0) == lax.broadcasted_iota(jnp.int32, (GROUP, LANES), 1)
+    ).astype(jnp.float32)
+    groups = TILE // GROUP
+
+    for q in range(chunks):
+        def arrived(j, carry):
+            far_copy(q, j).wait()
+            return carry
+
+        lax.fori_loop(1, half, arrived, 0)
+
+        def code(t, carry):
+            start = pl.multiple_of(t * TILE, 16)
+
+            def add(j, total):
+                return total + jnp.dot(
+                    hot[j, pl.ds(start, TILE)], got_far[q, j], preferred_element_type=jnp.float32
+                )
+
+            total = lax.fori_loop(0, half, add, jnp.zeros((TILE, LANES), jnp.float32))
+            largest = jnp.max(jnp.abs(total), axis=1, keepdims=True)
+            scale = largest * (1.0 / 32767.0)
+            factor = jnp.where(largest > 0.0, 32767.0 / jnp.where(largest > 0.0, largest, 1.0), 0.0)
+            whole = jnp.clip(jnp.floor(total * factor + 0.5), -32767.0, 32767.0)
+            coded[q, pl.ds(start, TILE)] = whole.astype(jnp.int32).astype(jnp.int16)
+            for u in range(groups):
+                flat = jnp.sum(scale[u * GROUP:(u + 1) * GROUP] * eye, axis=0, keepdims=True)
+                scales[q, pl.ds(t * groups + u, 1), :] = flat
+            return carry
+
+        lax.fori_loop(0, rows // TILE, code, 0)
+        scale_copy(q).start()
+        code_copy(q).start()
+        if q + 1 < chunks:
+            send_group(q + 1)
 
     @pl.when(me < n - 1)
     def _():
@@ -114,24 +219,37 @@
 
     def extend_add(numbers, block):
         def step(t, carry):
-            start = pl.multiple_of(t * tile, 16)
-            row = lax.broadcasted_iota(jnp.int32, (tile, numbers.shape[1]), 0) + start
-            hot = (row == numbers).astype(jnp.float32).astype(jnp.bfloat16)
-            sketch[pl.ds(start, tile)] += jnp.dot(hot, block, preferred_element_type=jnp.float32)
-            return carry
-
-        lax.fori_loop(0, rows // tile, step, 0)
-
-    extend_add(local_map(me), child_ref[jnp.maximum(inv_ref[me], 0)])
-
-    def receive(i, carry):
-        j = distance(i)
-        map_copy(j).wait()
-        row_copy(j).wait()
-        extend_add(got_maps[j], got_rows[j])
-        return carry
-
-    lax.fori_loop(1, n, receive, 0)
+            start = pl.multiple_of(t * TILE, 16)
+            row = lax.broadcasted_iota(jnp.int32, (TILE, padded), 0) + start
+            marks = (row == numbers).astype(jnp.float32).astype(jnp.bfloat16)
+            sketch[pl.ds(start, TILE)] += jnp.dot(marks, block, preferred_element_type=jnp.float32)
+            return carry
+
+        lax.fori_loop(0, rows // TILE, step, 0)
+
+    extend_add(local_map(me), child_ref[block_of(me)])
+
+    def receive(j, carry):
+        own_copy(j).wait()
+        extend_add(got_maps[j, 0], got_own[j])
+        return carry
+
+    lax.fori_loop(1, half, receive, 0)
+
+    for q in range(chunks):
+        scale_copy(q).wait()
+        code_copy(q).wait()
+
+        def decode(t, carry):
+            for u in range(groups):
+                start = pl.multiple_of(t * TILE + u * GROUP, 16)
+                flat = got_scales[q, pl.ds(t * groups + u, 1), :]
+                scale = jnp.sum(flat * eye, axis=1, keepdims=True)
+                part = got_coded[q, pl.ds(start, GROUP)].astype(jnp.int32).astype(jnp.float32) * scale
+                sketch[pl.ds(start, GROUP), q * LANES:(q + 1) * LANES] += part
+            return carry
+
+        lax.fori_loop(0, rows // TILE, decode, 0)
 
     def choose(i, carry):
         for u in range(8):
@@ -147,11 +265,11 @@
     own = chosen[parity]
 
     def cross(t, carry):
-        start = pl.multiple_of(t * tile, 16)
-        cross_ref[pl.ds(start, tile)] = dot_rows(sketch[pl.ds(start, tile)], own)
-        return carry
-
-    lax.fori_loop(0, rows // tile, cross, 0)
+        start = pl.multiple_of(t * TILE, 16)
+        cross_ref[pl.ds(start, TILE)] = dot_rows(sketch[pl.ds(start, TILE)], own)
+        return carry
+
+    lax.fori_loop(0, rows // TILE, cross, 0)
     pair_copy.wait()
     pair_ref[...] = chosen[...]
 
@@ -219,6 +337,8 @@
     vmem = pl.BlockSpec(memory_space=pltpu.VMEM)
     smem = pl.BlockSpec(memory_space=pltpu.SMEM)
     dma = pltpu.SemaphoreType.DMA
+    half, chunks = n // 2, columns // LANES
+    scale_rows = -(-rows // (GROUP * 8)) * 8
     cross, pair = pl.pallas_call(
         functools.partial(front_kernel, n),
         out_shape=(
@@ -228,17 +348,25 @@
         in_specs=[smem, smem, vmem, vmem, vmem],
         out_specs=(vmem, vmem),
         scratch_shapes=[
-            pltpu.VMEM((n, padded, columns), jnp.bfloat16),
-            pltpu.VMEM((n, padded, columns), jnp.bfloat16),
-            pltpu.VMEM((n, 1, padded), jnp.int32),
-            pltpu.VMEM((n, 1, padded), jnp.int32),
+            pltpu.VMEM((half, padded, columns), jnp.bfloat16),
+            pltpu.VMEM((half, padded, columns), jnp.bfloat16),
+            pltpu.VMEM((chunks, half, padded, LANES), jnp.bfloat16),
+            pltpu.VMEM((chunks, half, padded, LANES), jnp.bfloat16),
+            pltpu.VMEM((half, 2, 1, padded), jnp.int32),
+            pltpu.VMEM((half, 2, 1, padded), jnp.int32),
+            pltpu.VMEM((half, rows, padded), jnp.bfloat16),
+            pltpu.VMEM((chunks, rows, LANES), jnp.int16),
+            pltpu.VMEM((chunks, rows, LANES), jnp.int16),
+            pltpu.VMEM((chunks, scale_rows, LANES), jnp.float32),
+            pltpu.VMEM((chunks, scale_rows, LANES), jnp.float32),
             pltpu.VMEM((2, LINE_CELLS, columns), jnp.bfloat16),
             pltpu.VMEM((rows, columns), jnp.float32),
             pltpu.VMEM((2, rank, columns), jnp.float32),
-            dma((n,)), dma((n,)), dma((n,)), dma((n,)), dma((2,)), dma((2,)), dma, dma,
+            dma((half,)), dma((half,)), dma((chunks, half)), dma((chunks, half)), dma((half,)), dma((half,)),
+            dma((chunks,)), dma((chunks,)), dma((chunks,)), dma((chunks,)), dma((2,)), dma((2,)), dma, dma,
         ],
         compiler_params=pltpu.CompilerParams(
-            collective_id=0, has_side_effects=True, vmem_limit_bytes=48 * 1024 * 1024
+            collective_id=0, has_side_effects=True, vmem_limit_bytes=56 * 1024 * 1024
         ),
     )(inv, skel_leaf, child, maps, omega)
     picks = lax.dynamic_slice_in_dim(skel_upper, position // 2, 1, 0)[0]

time: 186 us -> 155 us (0.83)
  the two profiles are of different devices: /device:TPU:13 before, /device:TPU:29 now
where the time goes in v2:
time: 155 us
  Pallas kernels  150 us (97%)
  local copies, waits for them, and re-layouts  3.66 us (2%)
    pallas_call x1, Pallas kernels, local(): pl.pallas_call(functools.partial(front_kernel, n), out_shape=(jax.ShapeDt...  133 us
    pallas_call x1, Pallas kernels, local(): pl.pallas_call(solve_kernel, out_shape=(jax.ShapeDtypeStruct((rows, rank)...  16.8 us

profile of v2, /device:TPU:29, one launch (start us, length us, event | category | flops | bytes accessed | tf_op | source)
XLA Modules:
  0.0 155.0 jit_solution(3832002489818360636)
XLA Ops:
  0.6 0.0 copy-start
  0.7 0.7 copy-done
  1.3 0.8 reshape.47.map_ref
  2.1 0.0 copy-start.3
  2.2 0.2 and_reduce_fusion
  2.4 0.2 divide_reduce_fusion
  2.7 0.6 select_reduce_fusion.inv_ref
  3.3 0.0 copy-done.3
  3.3 132.8 %shard_map.76 = (f32[1600,128]{1,0:T(8,128)}, f32[2,128,512]{2,1,0:T(8,128)}) custom-call(s32[16]{0:T(128)} %select_reduce_fusion.inv_ref, s32[128]{0:T(128)} %skel_ref.1, bf16[8,400,512]{2,1,0:T(8,128)(2,1)} %bitcast.6, s32[8,1,400]{2,1,0:T(1,128)} %copy-done.3, bf16[1600,512]{1,0:T(8,128)(2,1)} %omega_ref.1), custom_call_target="tpu_custom_call" | custom-call | tf_op jit(solution)/shard_map/pallas_call | solution.py:342
  136.1 0.0 copy-start.1
  136.1 1.1 copy-done.1
  137.2 0.0 copy-start.2
  137.2 1.0 copy-done.2
  138.2 16.8 %shard_map.77 = (f32[1600,128]{1,0:T(8,128)}, f32[128,128]{1,0:T(8,128)}, f32[1600,128]{1,0:T(8,128)}) custom-call(s32[128]{0:T(128)S(1)} %dynamic-slice_bitcast_fusion.pick_ref, s32[1]{0:T(128)} %bitcast.1.side_ref, f32[1600,128]{1,0:T(8,128)S(1)} %copy-done.1, f32[256,512]{1,0:T(8,128)S(1)} %bitcast.5), custom_call_target="tpu_custom_call" | custom-call | tf_op jit(solution)/shard_map/pallas_call | solution.py:373
  (2 shorter events, 0.0 us)
Async XLA Ops:
  0.6 0.7 copy-start
  2.1 1.1 copy-start.3
  136.1 1.1 copy-start.1
  137.2 1.0 copy-start.2

commit v3 on v2

--- a/solution.py
+++ b/solution.py
@@ -217,26 +217,36 @@
             6.0 * here - above.astype(jnp.float32) - below.astype(jnp.float32) - left - right
         )
 
-    def extend_add(numbers, block):
+    mark(0, local_map(me))
+
+    def mark_own(j, carry):
+        mark(j, got_maps[j, 0])
+        return carry
+
+    lax.fori_loop(1, half, mark_own, 0)
+
+    def extend_add(j, block):
         def step(t, carry):
             start = pl.multiple_of(t * TILE, 16)
-            row = lax.broadcasted_iota(jnp.int32, (TILE, padded), 0) + start
-            marks = (row == numbers).astype(jnp.float32).astype(jnp.bfloat16)
-            sketch[pl.ds(start, TILE)] += jnp.dot(marks, block, preferred_element_type=jnp.float32)
+            sketch[pl.ds(start, TILE)] += jnp.dot(
+                hot[j, pl.ds(start, TILE)], block, preferred_element_type=jnp.float32
+            )
             return carry
 
         lax.fori_loop(0, rows // TILE, step, 0)
 
-    extend_add(local_map(me), child_ref[block_of(me)])
+    extend_add(0, child_ref[block_of(me)])
 
     def receive(j, carry):
         own_copy(j).wait()
-        extend_add(got_maps[j, 0], got_own[j])
-        return carry
-
-    lax.fori_loop(1, half, receive, 0)
+        extend_add(j, got_own[j])
+        return carry
+
+    lax.fori_loop(1, half - half // 4, receive, 0)
 
     for q in range(chunks):
+        if q == chunks // 2:
+            lax.fori_loop(half - half // 4, half, receive, 0)
         scale_copy(q).wait()
         code_copy(q).wait()
 
@@ -290,6 +300,26 @@
     return matrices
 
 
+def gram_blocks(rows):
+    half = rows.shape[0] // 2
+    top, low = rows[:half], rows[half:]
+    return dot_rows(top, top), dot_rows(top, low), dot_rows(low, top), dot_rows(low, low)
+
+
+def invert_grams(first, second):
+    blocks = [gram_blocks(first), gram_blocks(second)]
+    tops = invert_pair(blocks[0][0], blocks[1][0])
+    left = [exact_dot(b[2], p) for b, p in zip(blocks, tops)]
+    right = [exact_dot(p, b[1]) for b, p in zip(blocks, tops)]
+    lows = invert_pair(*[b[3] - exact_dot(v, b[1]) for b, v in zip(blocks, left)])
+    inverses = []
+    for p, q, v, w in zip(tops, lows, left, right):
+        low_left = -exact_dot(q, v)
+        top = jnp.concatenate([p - exact_dot(w, low_left), -exact_dot(w, q)], axis=1)
+        inverses.append(jnp.concatenate([top, jnp.concatenate([low_left, q], axis=1)], axis=0))
+    return inverses
+
+
 def solve_kernel(pick_ref, side_ref, cross_ref, pair_ref, leaf_ref, upper_ref, nested_ref, picked):
     rank = picked.shape[0]
     own = pair_ref[pl.ds(pl.multiple_of(side_ref[0] * rank, rank), rank), :]
@@ -301,7 +331,7 @@
 
     lax.fori_loop(0, rank // 8, pick, 0)
     upper_rows = picked[...]
-    leaf_inverse, upper_inverse = invert_pair(dot_rows(own, own), dot_rows(upper_rows, upper_rows))
+    leaf_inverse, upper_inverse = invert_grams(own, upper_rows)
     upper = exact_dot(dot_rows(own, upper_rows), upper_inverse)
     upper_ref[...] = upper
     tile = LINE_CELLS

time: 155 us -> 157 us (1.013)
  no operation moved by 1% of the time
where the time goes in v3:
time: 157 us; the launch traced here: 156 us
  Pallas kernels  151 us (96%)
  local copies, waits for them, and re-layouts  3.66 us (2%)
    pallas_call x1, Pallas kernels, local(): pl.pallas_call(functools.partial(front_kernel, n), out_shape=(jax.ShapeDt...  133 us
    pallas_call x1, Pallas kernels, local(): pl.pallas_call(solve_kernel, out_shape=(jax.ShapeDtypeStruct((rows, rank)...  18.1 us

profile of v3, /device:TPU:29, one launch (start us, length us, event | category | flops | bytes accessed | tf_op | source)
XLA Modules:
  0.0 156.4 jit_solution(16386885331106515546)
XLA Ops:
  0.6 0.0 copy-start
  0.7 0.7 copy-done
  1.3 0.8 reshape.47.map_ref
  2.1 0.0 copy-start.3
  2.2 0.2 and_reduce_fusion
  2.4 0.2 divide_reduce_fusion
  2.7 0.6 select_reduce_fusion.inv_ref
  3.3 0.0 copy-done.3
  3.3 132.8 %shard_map.76 = (f32[1600,128]{1,0:T(8,128)}, f32[2,128,512]{2,1,0:T(8,128)}) custom-call(s32[16]{0:T(128)} %select_reduce_fusion.inv_ref, s32[128]{0:T(128)} %skel_ref.1, bf16[8,400,512]{2,1,0:T(8,128)(2,1)} %bitcast.6, s32[8,1,400]{2,1,0:T(1,128)} %copy-done.3, bf16[1600,512]{1,0:T(8,128)(2,1)} %omega_ref.1), custom_call_target="tpu_custom_call" | custom-call | tf_op jit(solution)/shard_map/pallas_call | solution.py:372
  136.1 0.0 copy-start.1
  136.1 1.1 copy-done.1
  137.2 0.0 copy-start.2
  137.2 1.0 copy-done.2
  138.2 18.1 %shard_map.77 = (f32[1600,128]{1,0:T(8,128)}, f32[128,128]{1,0:T(8,128)}, f32[1600,128]{1,0:T(8,128)}) custom-call(s32[128]{0:T(128)S(1)} %dynamic-slice_bitcast_fusion.pick_ref, s32[1]{0:T(128)} %bitcast.1.side_ref, f32[1600,128]{1,0:T(8,128)S(1)} %copy-done.1, f32[256,512]{1,0:T(8,128)S(1)} %bitcast.5), custom_call_target="tpu_custom_call" | custom-call | tf_op jit(solution)/shard_map/pallas_call | solution.py:403
  (2 shorter events, 0.0 us)
Async XLA Ops:
  0.6 0.7 copy-start
  2.1 1.1 copy-start.3
  136.1 1.1 copy-start.1
  137.2 1.0 copy-start.2

commit v4 on v3

--- a/solution.py
+++ b/solution.py
@@ -11,6 +11,7 @@
 LANES = 128
 TILE = 320
 GROUP = 64
+PIVOTS = 4
 MESH = pl.DeviceIdType.MESH
 HIGHEST = lax.Precision.HIGHEST
 
@@ -26,7 +27,8 @@
 
 
 def front_kernel(
-    n, inv_ref, skel_ref, child_ref, map_ref, omega_ref, cross_ref, pair_ref,
+    n, inv_ref, skel_ref, child_hbm, map_ref, omega_hbm, cross_ref, pair_ref,
+    child_ref, omega_ref, child_sem, omega_sem,
     own_rows, got_own, far_rows, got_far, send_maps, got_maps, hot, coded, got_coded, scales, got_scales,
     halo, sketch, chosen,
     own_send, own_recv, far_send, far_recv, map_send, map_recv,
@@ -46,6 +48,10 @@
     partner = me + 1 - 2 * parity
     chunks = columns // LANES
 
+    child_copy = pltpu.make_async_copy(child_hbm, child_ref, child_sem)
+    child_copy.start()
+    omega_copy = pltpu.make_async_copy(omega_hbm, omega_ref, omega_sem)
+    omega_copy.start()
     halo[...] = jnp.zeros_like(halo)
     scales[...] = jnp.zeros_like(scales)
     barrier = pltpu.get_barrier_semaphore()
@@ -87,7 +93,7 @@
     def halo_copy(side):
         start = rows - LINE_CELLS if side == 0 else 0
         return pltpu.make_async_remote_copy(
-            omega_ref.at[pl.ds(start, LINE_CELLS)], halo.at[side], halo_send.at[side], halo_recv.at[side],
+            omega_hbm.at[pl.ds(start, LINE_CELLS)], halo.at[side], halo_send.at[side], halo_recv.at[side],
             device_id={"row": (me + 1) % n if side == 0 else (me + n - 1) % n}, device_id_type=MESH,
         )
 
@@ -123,6 +129,7 @@
         lax.fori_loop(low, high, send_own, 0)
 
     lax.fori_loop(1, half, send_map, 0)
+    child_copy.wait()
     send_far(0)
 
     @pl.when(me < n - 1)
@@ -205,6 +212,7 @@
         halo_copy(1).wait_send()
         halo_copy(0).wait_recv()
 
+    omega_copy.wait()
     cell = lax.broadcasted_iota(jnp.int32, (LINE_CELLS, columns), 0)
     lines = rows // LINE_CELLS
     for line in range(lines):
@@ -286,42 +294,42 @@
 
 def invert_pair(first, second):
     size = first.shape[0]
-    row_id = lax.broadcasted_iota(jnp.int32, (size, size), 0)
+    b = PIVOTS
     lane_id = lax.broadcasted_iota(jnp.int32, (size, size), 1)
+    eight = lax.broadcasted_iota(jnp.int32, (8, size), 0)
     matrices = [first, second]
-    for k in range(size):
+    for k in range(0, size, b):
+        pivots = (lane_id >= k) & (lane_id < k + b)
         for m in range(2):
             a = matrices[m]
-            scale = 1.0 / a[k:k + 1, k:k + 1]
-            row = jnp.where(lane_id[:1] == k, 1.0, a[k:k + 1, :]) * scale
-            column = a[:, k:k + 1]
-            rest = jnp.where(lane_id == k, 0.0, a) - column * row
-            matrices[m] = jnp.where(row_id == k, row, rest)
+            columns = [jnp.broadcast_to(a[:, k + i:k + i + 1], (size, size)) for i in range(b)]
+            small = [[columns[j][k + i:k + i + 1] for j in range(b)] for i in range(b)]
+            rows = [jnp.where(pivots[:1], (lane_id[:1] == k + i).astype(jnp.float32), a[k + i:k + i + 1]) for i in range(b)]
+            for p in range(b):
+                scale = 1.0 / small[p][p]
+                rows[p] = rows[p] * scale
+                for j in range(p + 1, b):
+                    small[p][j] = small[p][j] * scale
+                for i in range(b):
+                    if i != p:
+                        rows[i] = rows[i] - small[i][p] * rows[p]
+                        for j in range(p + 1, b):
+                            small[i][j] = small[i][j] - small[i][p] * small[p][j]
+            rest = jnp.where(pivots, 0.0, a)
+            for i in range(b):
+                rest = rest - columns[i] * rows[i]
+            at = k // 8 * 8
+            group = rest[at:at + 8]
+            for i in range(b):
+                group = jnp.where(eight == k + i - at, rows[i], group)
+            matrices[m] = jnp.concatenate([x for x in (rest[:at], group, rest[at + 8:]) if x.shape[0]], axis=0)
     return matrices
 
 
-def gram_blocks(rows):
-    half = rows.shape[0] // 2
-    top, low = rows[:half], rows[half:]
-    return dot_rows(top, top), dot_rows(top, low), dot_rows(low, top), dot_rows(low, low)
-
-
-def invert_grams(first, second):
-    blocks = [gram_blocks(first), gram_blocks(second)]
-    tops = invert_pair(blocks[0][0], blocks[1][0])
-    left = [exact_dot(b[2], p) for b, p in zip(blocks, tops)]
-    right = [exact_dot(p, b[1]) for b, p in zip(blocks, tops)]
-    lows = invert_pair(*[b[3] - exact_dot(v, b[1]) for b, v in zip(blocks, left)])
-    inverses = []
-    for p, q, v, w in zip(tops, lows, left, right):
-        low_left = -exact_dot(q, v)
-        top = jnp.concatenate([p - exact_dot(w, low_left), -exact_dot(w, q)], axis=1)
-        inverses.append(jnp.concatenate([top, jnp.concatenate([low_left, q], axis=1)], axis=0))
-    return inverses
-
-
-def solve_kernel(pick_ref, side_ref, cross_ref, pair_ref, leaf_ref, upper_ref, nested_ref, picked):
+def solve_kernel(pick_ref, side_ref, cross_hbm, pair_ref, leaf_ref, upper_ref, nested_ref, picked, cross_ref, cross_sem):
     rank = picked.shape[0]
+    cross_copy = pltpu.make_async_copy(cross_hbm, cross_ref, cross_sem)
+    cross_copy.start()
     own = pair_ref[pl.ds(pl.multiple_of(side_ref[0] * rank, rank), rank), :]
 
     def pick(i, carry):
@@ -331,10 +339,12 @@
 
     lax.fori_loop(0, rank // 8, pick, 0)
     upper_rows = picked[...]
-    leaf_inverse, upper_inverse = invert_grams(own, upper_rows)
+    leaf_inverse, upper_inverse = invert_pair(dot_rows(own, own), dot_rows(upper_rows, upper_rows))
     upper = exact_dot(dot_rows(own, upper_rows), upper_inverse)
     upper_ref[...] = upper
     tile = LINE_CELLS
+
+    cross_copy.wait()
 
     def finish(t, carry):
         start = pl.multiple_of(t * tile, 16)
@@ -366,6 +376,7 @@
     inv = jnp.max(jnp.where(targets[None, :] == places[:, None], numbers[None, :], -1), axis=1)
     vmem = pl.BlockSpec(memory_space=pltpu.VMEM)
     smem = pl.BlockSpec(memory_space=pltpu.SMEM)
+    anywhere = pl.BlockSpec(memory_space=pl.ANY)
     dma = pltpu.SemaphoreType.DMA
     half, chunks = n // 2, columns // LANES
     scale_rows = -(-rows // (GROUP * 8)) * 8
@@ -375,9 +386,12 @@
             jax.ShapeDtypeStruct((rows, rank), jnp.float32),
             jax.ShapeDtypeStruct((2, rank, columns), jnp.float32),
         ),
-        in_specs=[smem, smem, vmem, vmem, vmem],
+        in_specs=[smem, smem, anywhere, vmem, anywhere],
         out_specs=(vmem, vmem),
         scratch_shapes=[
+            pltpu.VMEM((blocks, padded, columns), jnp.bfloat16),
+            pltpu.VMEM((rows, columns), jnp.bfloat16),
+            dma, dma,
             pltpu.VMEM((half, padded, columns), jnp.bfloat16),
             pltpu.VMEM((half, padded, columns), jnp.bfloat16),
             pltpu.VMEM((chunks, half, padded, LANES), jnp.bfloat16),
@@ -407,10 +421,10 @@
             jax.ShapeDtypeStruct((rank, rank), jnp.float32),
             jax.ShapeDtypeStruct((rows, rank), jnp.float32),
         ),
-        in_specs=[smem, smem, vmem, vmem],
+        in_specs=[smem, smem, anywhere, vmem],
         out_specs=(vmem, vmem, vmem),
-        scratch_shapes=[pltpu.VMEM((rank, columns), jnp.float32)],
-        compiler_params=pltpu.CompilerParams(vmem_limit_bytes=32 * 1024 * 1024),
+        scratch_shapes=[pltpu.VMEM((rank, columns), jnp.float32), pltpu.VMEM((rows, rank), jnp.float32), dma],
+        compiler_params=pltpu.CompilerParams(vmem_limit_bytes=56 * 1024 * 1024),
     )(picks, (position % 2).reshape(1), cross, pair.reshape(2 * rank, columns))
 
 

time: 157 us -> 148 us (0.943)
  Pallas kernels: 151 us -> 144 us
  local copies, waits for them, and re-layouts: 3.66 us -> 2.06 us
    pallas_call x1, Pallas kernels: 18.1 us -> 12.9 us  [local(): pl.pallas_call(solve_kernel, out_shape=(jax.ShapeDtypeStruct((rows, rank)...]
    unnamed x8 -> x4, local copies, waits for them, and re-layouts: 2.85 us -> 0.67 us
    pallas_call x1, Pallas kernels: 133 us -> 131 us  [local(): pl.pallas_call(functools.partial(front_kernel, n), out_shape=(jax.ShapeDt...]
where the time goes in v4:
time: 148 us
  Pallas kernels  144 us (97%)
  local copies, waits for them, and re-layouts  2.06 us (1%)
    pallas_call x1, Pallas kernels, local(): pl.pallas_call(functools.partial(front_kernel, n), out_shape=(jax.ShapeDt...  131 us
    pallas_call x1, Pallas kernels, local(): pl.pallas_call(solve_kernel, out_shape=(jax.ShapeDtypeStruct((rows, rank)...  12.9 us

profile of v4, /device:TPU:29, one launch (start us, length us, event | category | flops | bytes accessed | tf_op | source)
XLA Modules:
  0.0 147.8 jit_solution(17149187924176623116)
XLA Ops:
  0.6 0.0 copy-start
  0.7 0.7 copy-done
  1.3 0.6 dynamic-slice_bitcast_fusion.pick_ref
  1.9 0.8 reshape.47.map_ref
  2.7 0.0 copy-start.1
  2.7 0.2 and_reduce_fusion
  3.0 0.2 divide_reduce_fusion
  3.2 0.6 select_reduce_fusion.inv_ref
  3.8 0.0 copy-done.1
  3.8 131.1 %shard_map.76 = (f32[1600,128]{1,0:T(8,128)}, f32[2,128,512]{2,1,0:T(8,128)}) custom-call(s32[16]{0:T(128)} %select_reduce_fusion.inv_ref, s32[128]{0:T(128)} %skel_ref.1, bf16[8,400,512]{2,1,0:T(8,128)(2,1)} %bitcast.5, s32[8,1,400]{2,1,0:T(1,128)} %copy-done.1, bf16[1600,512]{1,0:T(8,128)(2,1)} %omega_hbm.1), custom_call_target="tpu_custom_call" | custom-call | tf_op jit(solution)/shard_map/pallas_call | solution.py:383
  135.0 12.9 %shard_map.77 = (f32[1600,128]{1,0:T(8,128)}, f32[128,128]{1,0:T(8,128)}, f32[1600,128]{1,0:T(8,128)}) custom-call(s32[128]{0:T(128)} %dynamic-slice_bitcast_fusion.pick_ref, s32[1]{0:T(128)} %bitcast.1.side_ref, f32[1600,128]{1,0:T(8,128)} %get-tuple-element.5.cross_hbm, f32[256,512]{1,0:T(8,128)} %bitcast.6), custom_call_target="tpu_custom_call" | custom-call | tf_op jit(solution)/shard_map/pallas_call | solution.py:417
  (1 shorter events, 0.0 us)
Async XLA Ops:
  0.6 0.7 copy-start
  2.7 1.1 copy-start.1

commit v5 on v4

--- a/solution.py
+++ b/solution.py
@@ -27,8 +27,8 @@
 
 
 def front_kernel(
-    n, inv_ref, skel_ref, child_hbm, map_ref, omega_hbm, cross_ref, pair_ref,
-    child_ref, omega_ref, child_sem, omega_sem,
+    n, number_ref, skel_ref, child_hbm, map_ref, omega_hbm, cross_ref, pair_ref,
+    inv_ref, child_ref, omega_ref, child_sem, omega_sem,
     own_rows, got_own, far_rows, got_far, send_maps, got_maps, hot, coded, got_coded, scales, got_scales,
     halo, sketch, chosen,
     own_send, own_recv, far_send, far_recv, map_send, map_recv,
@@ -61,6 +61,18 @@
         return carry
 
     lax.fori_loop(1, n, greet, 0)
+    blocks = child_ref.shape[0]
+    slot = number_ref.shape[0] // blocks
+
+    def look_up(to, carry):
+        found = jnp.int32(-1)
+        for k in range(blocks):
+            first = number_ref[k * slot]
+            found = jnp.where((first >= to * rows) & (first < (to + 1) * rows), k, found)
+        inv_ref[to] = found
+        return carry
+
+    lax.fori_loop(0, n, look_up, 0)
     pl.semaphore_wait(barrier, n - 1)
 
     def peer_copy(source, target, send, recv, j):
@@ -326,15 +338,16 @@
     return matrices
 
 
-def solve_kernel(pick_ref, side_ref, cross_hbm, pair_ref, leaf_ref, upper_ref, nested_ref, picked, cross_ref, cross_sem):
+def solve_kernel(pick_ref, cross_hbm, pair_ref, leaf_ref, upper_ref, nested_ref, picked, cross_ref, cross_sem):
     rank = picked.shape[0]
     cross_copy = pltpu.make_async_copy(cross_hbm, cross_ref, cross_sem)
     cross_copy.start()
-    own = pair_ref[pl.ds(pl.multiple_of(side_ref[0] * rank, rank), rank), :]
+    me = lax.axis_index("row")
+    own = pair_ref[pl.ds(pl.multiple_of(me % 2 * rank, rank), rank), :]
 
     def pick(i, carry):
         for u in range(8):
-            picked[pl.ds(i * 8 + u, 1), :] = pair_ref[pl.ds(pick_ref[i * 8 + u], 1), :]
+            picked[pl.ds(i * 8 + u, 1), :] = pair_ref[pl.ds(pick_ref[me // 2, i * 8 + u], 1), :]
         return carry
 
     lax.fori_loop(0, rank // 8, pick, 0)
@@ -361,19 +374,14 @@
     rows, columns = omega.shape
     rank = skel_leaf.shape[0]
     n = lax.axis_size("row")
-    position = lax.axis_index("row")
     slot = 4 * rows // n
     blocks = child_sketch.shape[0] // slot
     padded = -(-slot // 16) * 16
     child = child_sketch.reshape(blocks, slot, columns)
     maps = child_map.reshape(blocks, 1, slot)
-    targets = maps[:, 0, 0] // rows
     if padded != slot:
         child = jnp.pad(child, ((0, 0), (0, padded - slot), (0, 0)))
         maps = jnp.pad(maps, ((0, 0), (0, 0), (0, padded - slot)), constant_values=-1)
-    numbers = jnp.arange(blocks, dtype=jnp.int32)
-    places = jnp.arange(n, dtype=jnp.int32)
-    inv = jnp.max(jnp.where(targets[None, :] == places[:, None], numbers[None, :], -1), axis=1)
     vmem = pl.BlockSpec(memory_space=pltpu.VMEM)
     smem = pl.BlockSpec(memory_space=pltpu.SMEM)
     anywhere = pl.BlockSpec(memory_space=pl.ANY)
@@ -389,6 +397,7 @@
         in_specs=[smem, smem, anywhere, vmem, anywhere],
         out_specs=(vmem, vmem),
         scratch_shapes=[
+            pltpu.SMEM((n,), jnp.int32),
             pltpu.VMEM((blocks, padded, columns), jnp.bfloat16),
             pltpu.VMEM((rows, columns), jnp.bfloat16),
             dma, dma,
@@ -412,8 +421,7 @@
         compiler_params=pltpu.CompilerParams(
             collective_id=0, has_side_effects=True, vmem_limit_bytes=56 * 1024 * 1024
         ),
-    )(inv, skel_leaf, child, maps, omega)
-    picks = lax.dynamic_slice_in_dim(skel_upper, position // 2, 1, 0)[0]
+    )(child_map, skel_leaf, child, maps, omega)
     return pl.pallas_call(
         solve_kernel,
         out_shape=(
@@ -421,11 +429,11 @@
             jax.ShapeDtypeStruct((rank, rank), jnp.float32),
             jax.ShapeDtypeStruct((rows, rank), jnp.float32),
         ),
-        in_specs=[smem, smem, anywhere, vmem],
+        in_specs=[smem, anywhere, vmem],
         out_specs=(vmem, vmem, vmem),
         scratch_shapes=[pltpu.VMEM((rank, columns), jnp.float32), pltpu.VMEM((rows, rank), jnp.float32), dma],
         compiler_params=pltpu.CompilerParams(vmem_limit_bytes=56 * 1024 * 1024),
-    )(picks, (position % 2).reshape(1), cross, pair.reshape(2 * rank, columns))
+    )(skel_upper, cross, pair.reshape(2 * rank, columns))
 
 
 def solution(mesh):

time: 148 us -> 147 us (level)
  no operation moved by 1% of the time
where the time goes in v5:
time: 147 us; the launch traced here: 146 us
  Pallas kernels  144 us (98%)
    pallas_call x1, Pallas kernels, local(): pl.pallas_call(functools.partial(front_kernel, n), out_shape=(jax.ShapeDt...  131 us
    pallas_call x1, Pallas kernels, local(): pl.pallas_call(solve_kernel, out_shape=(jax.ShapeDtypeStruct((rows, rank)...  13.1 us

profile of v5, /device:TPU:29, one launch (start us, length us, event | category | flops | bytes accessed | tf_op | source)
XLA Modules:
  0.0 146.4 jit_solution(11327977897096960255)
XLA Ops:
  0.6 1.4 reshape.16.map_ref
  2.0 131.3 %shard_map.76 = (f32[1600,128]{1,0:T(8,128)}, f32[2,128,512]{2,1,0:T(8,128)}) custom-call(s32[3200]{0:T(1024)} %number_ref.1, s32[128]{0:T(128)} %skel_ref.1, bf16[8,400,512]{2,1,0:T(8,128)(2,1)} %bitcast.2, s32[8,1,400]{2,1,0:T(1,128)} %reshape.16.map_ref, bf16[1600,512]{1,0:T(8,128)(2,1)} %omega_hbm.1), custom_call_target="tpu_custom_call" | custom-call | tf_op jit(solution)/shard_map/pallas_call | solution.py:391
  133.3 13.1 %shard_map.77 = (f32[1600,128]{1,0:T(8,128)}, f32[128,128]{1,0:T(8,128)}, f32[1600,128]{1,0:T(8,128)}) custom-call(s32[8,128]{1,0:T(8,128)} %pick_ref.1, f32[1600,128]{1,0:T(8,128)} %get-tuple-element.5.cross_hbm, f32[256,512]{1,0:T(8,128)} %bitcast.3), custom_call_target="tpu_custom_call" | custom-call | tf_op jit(solution)/shard_map/pallas_call | solution.py:425

commit v6 on v5

--- a/solution.py
+++ b/solution.py
@@ -265,7 +265,7 @@
     lax.fori_loop(1, half - half // 4, receive, 0)
 
     for q in range(chunks):
-        if q == chunks // 2:
+        if q == chunks - 1:
             lax.fori_loop(half - half // 4, half, receive, 0)
         scale_copy(q).wait()
         code_copy(q).wait()

time: 147 us -> 147 us (level)
  no operation moved by 1% of the time
where the time goes in v6:
time: 147 us; the launch traced here: 146 us
  Pallas kernels  144 us (98%)
    pallas_call x1, Pallas kernels, local(): pl.pallas_call(functools.partial(front_kernel, n), out_shape=(jax.ShapeDt...  131 us
    pallas_call x1, Pallas kernels, local(): pl.pallas_call(solve_kernel, out_shape=(jax.ShapeDtypeStruct((rows, rank)...  13.1 us

profile of v6, /device:TPU:29, one launch (start us, length us, event | category | flops | bytes accessed | tf_op | source)
XLA Modules:
  0.0 146.4 jit_solution(9176758011839895109)
XLA Ops:
  0.6 1.4 reshape.16.map_ref
  2.0 131.3 %shard_map.76 = (f32[1600,128]{1,0:T(8,128)}, f32[2,128,512]{2,1,0:T(8,128)}) custom-call(s32[3200]{0:T(1024)} %number_ref.1, s32[128]{0:T(128)} %skel_ref.1, bf16[8,400,512]{2,1,0:T(8,128)(2,1)} %bitcast.2, s32[8,1,400]{2,1,0:T(1,128)} %reshape.16.map_ref, bf16[1600,512]{1,0:T(8,128)(2,1)} %omega_hbm.1), custom_call_target="tpu_custom_call" | custom-call | tf_op jit(solution)/shard_map/pallas_call | solution.py:391
  133.3 13.1 %shard_map.77 = (f32[1600,128]{1,0:T(8,128)}, f32[128,128]{1,0:T(8,128)}, f32[1600,128]{1,0:T(8,128)}) custom-call(s32[8,128]{1,0:T(8,128)} %pick_ref.1, f32[1600,128]{1,0:T(8,128)} %get-tuple-element.5.cross_hbm, f32[256,512]{1,0:T(8,128)} %bitcast.3), custom_call_target="tpu_custom_call" | custom-call | tf_op jit(solution)/shard_map/pallas_call | solution.py:425
